TPU v7x, 128 devices: a whole 4x4x4 slice. The times are simulated.
128 devices in a mesh: row: 8 (over y, core), col: 16 (over x, z).
Axes of the slice: x: 4, y: 4, z: 4, core: 2. Of those that a mesh axis runs over, the one named last changes fastest.
Arguments:
- root_factor: float32 [4096, 4096], P('col')
- mid_factor: float32 [2, 1024, 1024], P(None, 'col')
- low_factor: float32 [4, 512, 512], P(None, 'col')
- mid_rows: float32 [2, 4096, 1024], P(None, 'row', 'col'), may hold values from -0.125 to 0.125
- low_parent_rows: float32 [4, 1024, 512], P(None, 'row', 'col'), may hold values from -0.109375 to 0.109375
- low_root_rows: float32 [4, 4096, 512], P(None, 'row', 'col'), may hold values from -0.109375 to 0.109375
- mid_struct: int32 [2, 10], replicated, may hold values from 0 to 15, all different within a row
- low_struct: int32 [4, 12], replicated, may hold values from 0 to 19, all different within a row
- low_parent: int32 [4], replicated, may hold values from 0 to 1
Outputs:
- root_sigma: float32 [4096, 4096], P('row', 'col')
- mid_diag: float32 [2, 1024, 1024], P(None, 'row', 'col')
- mid_cross: float32 [2, 1024, 4096], P(None, 'row', 'col')
- low_diag: float32 [4, 512, 512], P(None, 'row', 'col')
- low_cross_parent: float32 [4, 512, 1024], P(None, 'row', 'col')
- low_cross_root: float32 [4, 512, 4096], P(None, 'row', 'col')
Inputs may be any that keep to these rules, and one draw needn't show every extreme that they name: `mid_struct`: each row lists 10 different root blocks; every root block is listed by some row. `low_struct`: each row lists 12 different ancestor blocks; every block is listed by some row.
All inputs are finite; a program needn't handle non-finite values.
Results may differ from a plain program's by a relative error of at most 0.0001.
Values sent between devices are 32-bit elements; how exact they have to be, the bound alone decides.
A program may use at most 128 MiB of HBM per device.

v0:
```python
import functools

import jax
import jax.numpy as jnp
from jax import lax
from jax.experimental import pallas as pl
from jax.experimental.pallas import tpu as pltpu
from jax.sharding import PartitionSpec as P

BLOCK = 256
ROOT = 4096
MID = 1024
LOW = 512
MIDS = 2
LOWS = 4
MESH = pl.DeviceIdType.MESH
F32 = jnp.float32
VMEM = pltpu.VMEM
ANY = pl.ANY


class Net:
    def __init__(self, send_sem, recv_sem):
        self.row = lax.axis_index("row")
        self.col = lax.axis_index("col")
        self.place = {
            "x": lax.div(self.col, 4),
            "z": lax.rem(self.col, 4),
            "y": lax.div(self.row, 2),
            "core": lax.rem(self.row, 2),
        }
        self.send_sem, self.recv_sem, self.used, self.started = send_sem, recv_sem, 0, []

    def at(self, axis, shift):
        if axis == "core":
            return lax.rem(self.place["core"] + shift, 2)
        return lax.rem(self.place[axis] + shift + 4, 4)

    def device(self, **shifts):
        at = {axis: self.at(axis, shifts.get(axis, 0)) for axis in self.place}
        return (at["y"] * 2 + at["core"], at["x"] * 4 + at["z"])

    def greet(self, axes):
        barrier = pltpu.get_barrier_semaphore()
        count = 0
        for axis in axes:
            for shift in (1,) if axis == "core" else (1, -1):
                pl.semaphore_signal(barrier, inc=1, device_id=self.device(**{axis: shift}), device_id_type=MESH)
                count += 1
        pl.semaphore_wait(barrier, count)

    def send(self, src, dst, axis, shift):
        index = self.used
        self.used += 1
        copy = pltpu.make_async_remote_copy(
            src_ref=src,
            dst_ref=dst,
            send_sem=self.send_sem.at[index],
            recv_sem=self.recv_sem.at[index],
            device_id=self.device(**{axis: shift}),
            device_id_type=MESH,
        )
        copy.start()
        self.started.append(copy)
        return copy

    def finish(self):
        for copy in self.started:
            copy.wait_send()


def mult(value, unit):
    return pl.multiple_of(value, unit)


def params(collective_id):
    return pltpu.CompilerParams(collective_id=collective_id, has_side_effects=True, vmem_limit_bytes=60 * 2**20)


class Gather:
    def __init__(self, net, src, dst, whole, half, first, second, local_sem, share=None):
        self.net, self.dst, self.whole, self.half = net, dst, whole, half
        self.first, self.second, self.share = first, second, share
        self.src, self.local_sem = src, local_sem

    def spot(self, a, b):
        at = {self.first: self.net.at(self.first, a), self.second: self.net.at(self.second, b)}
        return at["x"], at["z"]

    def piece(self, a, b):
        return self.whole(self.dst, *self.spot(a, b))

    def part(self, a, b, h):
        return self.half(self.dst, *self.spot(a, b), h)

    def start(self):
        net, own = self.net, self.piece(0, 0)
        self.local = pltpu.make_async_copy(self.src, own, self.local_sem)
        self.local.start()
        self.p1 = [net.send(self.src, own, self.first, s) for s in (1, -1)]
        self.p2 = {0: [net.send(self.src, own, self.second, s) for s in (1, -1)]}

    def onward(self, a):
        piece = self.piece(a, 0)
        self.p2[a] = [self.net.send(piece, piece, self.second, s) for s in (1, -1)]

    def first_ring(self):
        self.fwd = []
        for index, shift in enumerate((1, -1)):
            self.p1[index].wait_recv()
            part = self.part(-shift, 0, index)
            self.fwd.append(self.net.send(part, part, self.first, shift))
            self.onward(-shift)

    def first_end(self):
        for copy in self.fwd:
            copy.wait_recv()
        self.onward(2)

    def second_ring(self, a):
        copies = []
        for index, shift in enumerate((1, -1)):
            self.p2[a][index].wait_recv()
            part = self.part(a, -shift, index)
            copies.append(self.net.send(part, part, self.second, shift))
        self.p2[a] = copies

    def second_end(self, a):
        for copy in self.p2[a]:
            copy.wait_recv()

    def finish(self):
        self.local.wait()


class Scatter:
    def __init__(self, net, axis, part, near, far):
        self.net, self.axis, self.part, self.near, self.far = net, axis, part, near, far

    def start(self):
        opposite = self.net.at(self.axis, 2)
        self.first = [
            self.net.send(self.part(opposite, h), self.near[h], self.axis, shift) for h, shift in enumerate((1, -1))
        ]
        self.second = [
            self.net.send(self.part(self.net.at(self.axis, shift), 1 - h), self.far[h][1 - h], self.axis, shift)
            for h, shift in enumerate((1, -1))
        ]

    def middle(self):
        for h, shift in enumerate((1, -1)):
            self.first[h].wait_recv()
            self.near[h][...] += self.part(self.net.at(self.axis, shift), h)[...]
            self.second.append(self.net.send(self.near[h], self.far[h][h], self.axis, shift))

    def end(self, out):
        for copy in self.second:
            copy.wait_recv()
        for h in range(2):
            out[h][...] = self.part(self.net.at(self.axis, 0), h)[...] + self.far[0][h][...] + self.far[1][h][...]


class TorusScatter:
    def __init__(self, net, part_xz, part_zx, bufs_xz, bufs_zx):
        self.net, self.bufs = net, (bufs_xz, bufs_zx)
        self.stages = [self.stage(axis, part, bufs[0], bufs[1])
                       for axis, part, bufs in (("x", part_xz, bufs_xz), ("z", part_zx, bufs_zx))]

    def stage(self, axis, part, near, far):
        return Scatter(self.net, axis, part, [near.at[0], near.at[1]], [[far.at[s, h] for h in range(2)] for s in range(2)])

    def start(self):
        for stage in self.stages:
            stage.start()

    def middle(self):
        for stage in self.stages:
            stage.middle()

    def turn(self):
        later = []
        for stage, axis, bufs in zip(self.stages, ("z", "x"), self.bufs):
            sums = bufs[2]
            stage.end([sums.at[0], sums.at[1]])
            part = functools.partial(lambda sums, o, h: sums.at[h, o], sums)
            later.append(self.stage(axis, part, bufs[3], bufs[4]))
            later[-1].start()
        self.stages = later

    second_middle = middle

    def end(self, out_xz, out_zx):
        for stage, out in zip(self.stages, (out_xz, out_zx)):
            stage.end(out)


def torus_bufs(rows, lanes):
    return [
        VMEM((2, 4, rows, lanes), F32),
        VMEM((2, 2, 4, rows, lanes), F32),
        VMEM((2, 4, rows, lanes), F32),
        VMEM((2, rows, lanes), F32),
        VMEM((2, 2, rows, lanes), F32),
    ]


def split(a):
    high = a.astype(jnp.bfloat16)
    return high, (a - high.astype(F32)).astype(jnp.bfloat16)


def dot3(a, b):
    go = functools.partial(jnp.dot, preferred_element_type=F32)
    return go(a[0], b[0]) + (go(a[0], b[1]) + go(a[1], b[0]))


class Ring:
    def __init__(self, net, pieces, halves):
        self.net, self.pieces, self.halves = net, pieces, halves

    def pair_up(self, place):
        self.pair += [self.net.send(part, part, "core", 1) for part in self.pieces(place)]

    def start(self):
        own = self.pieces(self.net.at("y", 0))
        self.near = [[self.net.send(part, part, "y", s) for part in own] for s in (1, -1)]
        self.pair = []
        self.pair_up(self.net.at("y", 0))

    def middle(self):
        self.far = []
        for index, shift in enumerate((1, -1)):
            for copy in self.near[index]:
                copy.wait_recv()
            place = self.net.at("y", -shift)
            self.far += [self.net.send(part, part, "y", shift) for part in self.halves(place, index)]
            self.pair_up(place)

    def end(self):
        for copy in self.far:
            copy.wait_recv()
        self.pair_up(self.net.at("y", 2))

    def finish(self):
        for copy in self.pair:
            copy.wait_recv()


def first_kernel(lr, m, r, p, lm, ll, sigma, m_all, r_all, q_all, lm_all, ll_all, p_all, q_own, terms, *scratch):
    bufs_xz, bufs_zx, (send_sem, recv_sem, local_sem) = scratch[:5], scratch[5:10], scratch[10:]
    net = Net(send_sem, recv_sem)
    net.greet(("x", "z", "y", "core"))
    core, y = net.place["core"], net.place["y"]

    def rows(x, z, n):
        return pl.ds(mult((x * 4 + z) * n, n), n)

    def eighth(n):
        return pl.ds(mult(y * n, n), n)

    two = pl.ds(2 * core, 2)
    ga_p = Gather(
        net, p, p_all,
        lambda ref, x, z: ref.at[:, rows(x, z, 32), :],
        lambda ref, x, z, h: ref.at[pl.ds(2 * h, 2), rows(x, z, 32), :],
        "x", "z", local_sem.at[0],
    )
    ga_ll = Gather(
        net, ll.at[two, eighth(8), :], ll_all,
        lambda ref, x, z: ref.at[two, x * 4 + z, eighth(8), :],
        lambda ref, x, z, h: ref.at[2 * core + h, x * 4 + z, eighth(8), :],
        "z", "x", local_sem.at[1],
    )
    ga_lm = Gather(
        net, lm.at[core, eighth(16), :], lm_all,
        lambda ref, x, z: ref.at[core, x * 4 + z, eighth(16), :],
        lambda ref, x, z, h: ref.at[core, x * 4 + z, pl.ds(mult(y * 16 + 8 * h, 8), 8), :],
        "x", "z", local_sem.at[2],
    )
    ga_m = Gather(
        net, m, m_all,
        lambda ref, x, z: ref.at[:, rows(x, z, 64), :],
        lambda ref, x, z, h: ref.at[h, rows(x, z, 64), :],
        "x", "z", local_sem.at[3],
    )
    ga_r = Gather(
        net, r, r_all,
        lambda ref, x, z: ref.at[:, rows(x, z, 32), :],
        lambda ref, x, z, h: ref.at[pl.ds(2 * h, 2), rows(x, z, 32), :],
        "z", "x", local_sem.at[4],
    )
    small, large = (ga_p, ga_ll, ga_lm), (ga_m, ga_r)
    def ll_parts(o):
        return [ll_all.at[two, pl.ds(8 * g, 8), pl.ds(mult(o * 8, 8), 8), pl.ds(0, 256 * (g + 1))] for g in range(2)]

    def lm_parts(o):
        return [
            lm_all.at[core, pl.ds(4 * g, 4), pl.ds(mult(o * 16, 16), 16), pl.ds(0, 256 * (g + 1))] for g in range(4)
        ]

    def q_lanes(o):
        return pl.ds(mult((2 * o + core) * 128, 128), 128)

    ring_ll = Ring(net, ll_parts, lambda o, h: ll_parts(o)[1:] if h else ll_parts(o)[:1])
    ring_lm = Ring(net, lm_parts, lambda o, h: lm_parts(o)[:3] if h else lm_parts(o)[3:])
    ring_q = Ring(net, lambda o: [q_all.at[:, :, q_lanes(o)]], lambda o, h: [q_all.at[pl.ds(2 * h, 2), :, q_lanes(o)]])

    for item in small + large:
        item.start()

    base = net.col * 256

    def lower(first, width):
        at = lambda axis: lax.broadcasted_iota(jnp.int32, (256, width), axis)
        return jnp.where(first + at(1) <= base + at(0), lr[:, pl.ds(mult(first, 128), width)], 0.0)

    left = split(jnp.transpose(lower(net.row * 512, 512)))

    @pl.loop(0, 16)
    def _(block):
        terms[lax.div(block, 4), lax.rem(block, 4)] = dot3(left, split(lower(block * 256, 256)))

    sc = TorusScatter(
        net,
        lambda o, h: terms.at[o, :, pl.ds(128 * h, 128), :],
        lambda o, h: terms.at[:, o, pl.ds(256 + 128 * h, 128), :],
        bufs_xz, bufs_zx,
    )
    sc.start()
    for item in small:
        item.first_ring()
    for item in small:
        item.first_end()
    for a in (0, -1, 1, 2):
        for item in small:
            item.second_ring(a)
    for item in large:
        item.first_ring()
    for item in small:
        for a in (0, -1, 1, 2):
            item.second_end(a)
        item.finish()
    ring_ll.start()
    ring_lm.start()
    for item in large:
        item.first_end()
    sc.middle()
    ring_ll.middle()
    for item in large:
        item.second_ring(0)
    ring_ll.end()
    ring_ll.finish()
    exact = functools.partial(jnp.dot, preferred_element_type=F32, precision=lax.Precision.HIGHEST)
    for i in range(LOWS):
        pt = jnp.transpose(p_all[i])
        q_own[i, :256] = jnp.transpose(exact(pt, ll_all[i, :, :, :256].reshape(LOW, 256)))
        q_own[i, 256:] = jnp.transpose(exact(pt[:, 256:], ll_all[i, 8:, :, 256:].reshape(256, 256)))
    local_q = pltpu.make_async_copy(q_own, q_all.at[:, :, q_lanes(y)], local_sem.at[5])
    local_q.start()
    for a in (-1, 1):
        for item in large:
            item.second_ring(a)
    local_q.wait()
    ring_q.start()
    sc.turn()
    ring_lm.middle()
    for item in large:
        item.second_ring(2)
    sc.second_middle()
    ring_q.middle()
    ring_lm.end()
    outs = lambda base: [sigma.at[pl.ds(base + 128 * h, 128), :] for h in range(2)]
    sc.end(outs(0), outs(256))
    for item in large:
        for a in (0, -1, 1, 2):
            item.second_end(a)
        item.finish()
    ring_q.end()
    ring_lm.finish()
    ring_q.finish()
    net.finish()


def first_step(lr, m, r, p, lm, ll):
    shape = lambda *dims: jax.ShapeDtypeStruct(dims, F32)
    vmem, hbm = pl.BlockSpec(memory_space=VMEM), pl.BlockSpec(memory_space=ANY)
    return pl.pallas_call(
        first_kernel,
        out_shape=(
            shape(512, 256), shape(MIDS, MID, 512), shape(LOWS, LOW, 512), shape(LOWS, LOW, MID),
            shape(MIDS, 16, 64, MID), shape(LOWS, 16, 32, LOW),
        ),
        in_specs=[vmem] + [hbm] * 5,
        out_specs=[vmem, hbm, hbm, hbm, hbm, vmem],
        scratch_shapes=[VMEM((LOWS, LOW, 128), F32), VMEM((LOWS, LOW, 128), F32), VMEM((4, 4, 512, 256), F32)]
        + torus_bufs(128, 256) + torus_bufs(128, 256) + [
            pltpu.SemaphoreType.DMA((220,)),
            pltpu.SemaphoreType.DMA((220,)),
            pltpu.SemaphoreType.DMA((8,)),
        ],
        compiler_params=params(0),
        name="first_step",
    )(lr, m, r, p, lm, ll)


CHUNKS = 4
STEP = 256


class Spread:
    def __init__(self, net, source, out, send_sem, recv_sem, local_sem):
        self.net, self.source, self.out = net, source, out
        self.send_sem, self.recv_sem, self.local_sem = send_sem, recv_sem, local_sem
        x, z = net.place["x"], net.place["z"]
        self.lanes = pl.ds(mult(lax.rem(z, 2) * 256, 256), 256)
        self.away = lax.rem(net.place["y"] - x + 4, 4)
        self.is_core = net.place["core"] == lax.div(z, 2)

    def spot(self, ref, way, chunk, lanes):
        per = ref.shape[1] // STEP
        return ref.at[way * (ref.shape[0] // 2) + chunk // per, pl.ds(chunk % per * STEP, STEP), lanes]

    def copy(self, way, chunk, pair, first=False):
        place = self.spot(self.out, way, chunk, slice(None))
        index = pair * 2 * CHUNKS + way * CHUNKS + chunk
        to = {"core": 1} if pair else {"y": 1 - 2 * way}
        return pltpu.make_async_remote_copy(
            src_ref=self.spot(self.source, way, chunk, self.lanes) if first else place, dst_ref=place,
            send_sem=self.send_sem.at[index], recv_sem=self.recv_sem.at[index],
            device_id=self.net.device(**to), device_id_type=MESH,
        )

    def load(self):
        return pltpu.make_async_copy(self.source.at[:, :, self.lanes], self.out, self.local_sem)

    def start(self):
        @pl.when(jnp.logical_and(self.is_core, self.away == 0))
        def _():
            self.load().start()
            for chunk in range(CHUNKS):
                for way in range(2):
                    self.copy(way, chunk, 0, True).start()
            for chunk in range(CHUNKS):
                for way in range(2):
                    self.copy(way, chunk, 1, True).start()

    def onward(self, first, last):
        for away in (1, 2, 3):
            @pl.when(jnp.logical_and(self.is_core, self.away == away))
            def _():
                for step in range(first, last):
                    for way in range(2):
                        hops = away if way == 0 else 4 - away
                        chunk = step + 1 - hops
                        if 0 <= chunk < CHUNKS:
                            self.copy(way, chunk, 0).wait_recv()
                            if hops < 3:
                                self.copy(way, chunk, 0).start()
                            self.copy(way, chunk, 1).start()

    def finish(self):
        @pl.when(jnp.logical_and(self.is_core, self.away == 0))
        def _():
            self.load().wait()

        for chunk in range(CHUNKS):
            for way in range(2):
                @pl.when(jnp.logical_and(self.is_core, self.away != (3, 1)[way]))
                def _():
                    self.copy(way, chunk, 0).wait_send()

                @pl.when(self.is_core)
                def _():
                    self.copy(way, chunk, 1).wait_send()

                @pl.when(jnp.logical_not(self.is_core))
                def _():
                    self.copy(way, chunk, 1).wait_recv()


def dot3_nt(a, b):
    go = lambda s, t: lax.dot_general(s, t, (((1,), (1,)), ((), ())), preferred_element_type=F32)
    return go(a[0], b[0]) + (go(a[0], b[1]) + go(a[1], b[0]))


def second_kernel(parent, sigma, lm_own, m_all, r_all, q_all, lm_all, ll_all, out_m, out_l, um_c, ul_c, g,
                  m, r, q, lm, ll, high, low, s_high, s_low, cm, cl, acc_m, acc_l, core_m, core_l, near_m, near_l,
                  far_m, far_l, send_sem, recv_sem, spread_send, spread_recv, local_sem):
    loads = [
        pltpu.make_async_copy(src, dst, local_sem.at[index])
        for index, (src, dst) in enumerate(((lm_all, lm), (m_all, m), (ll_all, ll), (r_all, r), (q_all, q)))
    ]
    for load in loads:
        load.start()
    net = Net(send_sem, recv_sem)
    net.greet(("y", "core"))
    core = net.place["core"]
    other = 1 - core
    s_high[...], s_low[...] = split(sigma[...])
    halves = lambda: (s_high[...], s_low[...])

    def band(block):
        return pl.ds(block * 256, 256)

    loads[0].wait()
    loads[1].wait()

    @pl.loop(0, MIDS)
    def _(p):
        for j in range(4):
            total = None
            for k in range(j, 4):
                tile = jnp.transpose(lm[p, pl.ds(4 * k, 4), :, band(j)].reshape(256, 256))
                term = dot3(split(tile), split(m[p, band(k), :]))
                total = term if total is None else total + term
            m[p, band(j), :] = total
            both = split(total)
            high[p, band(j), :], low[p, band(j), :] = both
            cm[p, band(j), :] = -dot3(both, halves())

    def slab(ref, rows, y, k):
        return ref.at[:, pl.ds(mult((2 * y + k) * rows, rows), rows), :]

    pair_m = {d: net.send(slab(cm, 128, net.at("y", d), other), core_m.at[d % 4], "core", 1) for d in (2, 1, -1, 0)}
    spread_m = Spread(net, m, um_c, spread_send.at[0], spread_recv.at[0], local_sem.at[5])
    spread_m.start()
    for load in loads[2:]:
        load.wait()

    def low_nodes(first):
        @pl.loop(first, first + 2)
        def _(i):
            p = parent[i]
            own = split(lm_own[p])
            for j in range(2):
                total = None
                for k in range(j, 2):
                    tile = jnp.transpose(ll[i, pl.ds(8 * k, 8), :, band(j)].reshape(256, 256))
                    term = dot3(split(tile), split(r[i, band(k), :]))
                    total = term if total is None else total + term
                q_both = split(q[i, band(j), :])
                total = total - dot3(q_both, (high[p], low[p]))
                g[i, band(j), :] = dot3_nt(q_both, own)
                r[i, band(j), :] = total
                cl[i, band(j), :] = -dot3(split(total), halves())

    low_nodes(0)
    spread_m.onward(0, 3)
    low_nodes(2)
    pair_l = {d: net.send(slab(cl, 64, net.at("y", d), other), core_l.at[d % 4], "core", 1) for d in (2, 1, -1, 0)}
    spread_m.onward(3, CHUNKS + 2)
    firsts = []
    spread_l = Spread(net, r, ul_c, spread_send.at[1], spread_recv.at[1], local_sem.at[6])
    for d in (2, 1, -1, 0):
        y = net.at("y", d)
        slot = d % 4
        pair_m[d].wait_recv()
        acc_m[slot] = core_m[slot] + slab(cm, 128, y, core)[...]
        pair_l[d].wait_recv()
        acc_l[slot] = core_l[slot] + slab(cl, 64, y, core)[...]
        if d == 2:
            firsts = [net.send(acc_m.at[2], near_m, "y", 1), net.send(acc_l.at[2], near_l, "y", -1)]
    seconds = [net.send(acc_l.at[1], far_l.at[0], "y", 1), net.send(acc_m.at[3], far_m.at[1], "y", -1)]
    spread_l.start()
    firsts[0].wait_recv()
    near_m[...] += acc_m[1]
    seconds.append(net.send(near_m, far_m.at[0], "y", 1))
    firsts[1].wait_recv()
    near_l[...] += acc_l[3]
    seconds.append(net.send(near_l, far_l.at[1], "y", -1))
    spread_l.onward(0, CHUNKS + 2)
    for copy in seconds:
        copy.wait_recv()
    out_m[...] = acc_m[0] + far_m[0] + far_m[1]
    out_l[...] = acc_l[0] + far_l[0] + far_l[1]
    spread_m.finish()
    spread_l.finish()
    net.finish()


def second_step(parent, sigma, lm, m_all, r_all, q_all, lm_all, ll_all):
    shape = lambda *dims: jax.ShapeDtypeStruct(dims, F32)
    vmem, hbm = pl.BlockSpec(memory_space=VMEM), pl.BlockSpec(memory_space=ANY)
    block = lambda *dims: VMEM(dims, F32)
    half = lambda *dims: VMEM(dims, jnp.bfloat16)
    return pl.pallas_call(
        second_kernel,
        out_shape=(
            shape(MIDS, 128, 256), shape(LOWS, 64, 256), shape(MIDS, MID, 256), shape(LOWS, LOW, 256), shape(LOWS, LOW, 64),
        ),
        in_specs=[pl.BlockSpec(memory_space=pltpu.SMEM), vmem, vmem] + [hbm] * 5,
        out_specs=[vmem] * 5,
        scratch_shapes=[
            block(MIDS, MID, 512), block(LOWS, LOW, 512), block(LOWS, LOW, MID), block(MIDS, 16, 64, MID),
            block(LOWS, 16, 32, LOW), half(MIDS, MID, 512), half(MIDS, MID, 512), half(512, 256), half(512, 256),
            block(MIDS, MID, 256), block(LOWS, LOW, 256),
            block(4, MIDS, 128, 256), block(4, LOWS, 64, 256), block(4, MIDS, 128, 256), block(4, LOWS, 64, 256),
            block(MIDS, 128, 256), block(LOWS, 64, 256), block(2, MIDS, 128, 256), block(2, LOWS, 64, 256),
            pltpu.SemaphoreType.DMA((24,)),
            pltpu.SemaphoreType.DMA((24,)),
            pltpu.SemaphoreType.DMA((2, 4 * CHUNKS)),
            pltpu.SemaphoreType.DMA((2, 4 * CHUNKS)),
            pltpu.SemaphoreType.DMA((8,)),
        ],
        compiler_params=params(1),
        name="second_step",
    )(parent, sigma, lm, m_all, r_all, q_all, lm_all, ll_all)


DIAG_ROWS = 320


def third_kernel(parent, mid_cross, low_root, um, ul, g, lm, ll, out, terms, lm_t, ll_t, *scratch):
    bufs_xz, bufs_zx, (send_sem, recv_sem) = scratch[:5], scratch[5:10], scratch[10:]
    net = Net(send_sem, recv_sem)
    net.greet(("x", "z"))
    for p in range(MIDS):
        lm_t[p] = jnp.transpose(lm[p])
    for i in range(LOWS):
        ll_t[i] = jnp.transpose(ll[i])
    low_rows = pl.ds(mult(net.row * 64, 64), 64)
    for p in range(MIDS):
        mine = split(lm_t[p, pl.ds(mult(net.row * 128, 128), 128), :])
        term = dot3_nt(split(lm_t[p]), mine) - dot3_nt(split(um[p]), split(mid_cross[p]))
        terms[:, :, pl.ds(64 * p, 64), :] = term.reshape(4, 4, 64, 128)
    for pair in range(2):
        par, own = [], []
        for i in (2 * pair, 2 * pair + 1):
            p = parent[i]
            root, g_mine = split(low_root[i]), split(g[i, low_rows, :])
            par.append(-(dot3_nt(split(um[p]), root) + dot3_nt(split(lm_t[p]), g_mine)))
            own.append(
                dot3_nt(split(ll_t[i]), split(ll_t[i, low_rows, :])) + dot3_nt(split(g[i]), g_mine)
                - dot3_nt(split(ul[i]), root)
            )
        terms[:, :, pl.ds(128 + 64 * pair, 64), :] = jnp.concatenate(par, axis=1).reshape(4, 4, 64, 128)
        terms[:, :, pl.ds(256 + 32 * pair, 32), :] = jnp.concatenate(own, axis=1).reshape(4, 4, 32, 128)
    half = DIAG_ROWS // 4

    def outs(base):
        return [out.at[pl.ds(base + half * h, half), :] for h in range(2)]

    sc = TorusScatter(
        net,
        lambda o, h: terms.at[o, :, pl.ds(half * h, half), :],
        lambda o, h: terms.at[:, o, pl.ds(2 * half + half * h, half), :],
        bufs_xz, bufs_zx,
    )
    sc.start()
    sc.middle()
    sc.turn()
    sc.second_middle()
    sc.end(outs(0), outs(2 * half))
    net.finish()


def third_step(parent, *arrays):
    return pl.pallas_call(
        third_kernel,
        out_shape=jax.ShapeDtypeStruct((DIAG_ROWS, 128), F32),
        in_specs=[pl.BlockSpec(memory_space=pltpu.SMEM)] + [pl.BlockSpec(memory_space=VMEM)] * 7,
        out_specs=pl.BlockSpec(memory_space=VMEM),
        scratch_shapes=[
            VMEM((4, 4, DIAG_ROWS, 128), F32), VMEM((MIDS, MID, 64), F32), VMEM((LOWS, LOW, 32), F32),
        ] + torus_bufs(DIAG_ROWS // 4, 128) + torus_bufs(DIAG_ROWS // 4, 128) + [
            pltpu.SemaphoreType.DMA((32,)),
            pltpu.SemaphoreType.DMA((32,)),
        ],
        compiler_params=params(2),
        name="third_step",
    )(parent, *arrays)


def lower_part(factor):
    rows_here = factor.shape[1]
    row_ids = lax.axis_index("col") * rows_here + lax.broadcasted_iota(jnp.int32, factor.shape[1:], 0)
    col_ids = lax.broadcasted_iota(jnp.int32, factor.shape[1:], 1)
    return jnp.where((col_ids <= row_ids)[None], factor, 0.0)


def live_mask(local_rows, first_row, structure, block_shift):
    row_ids = first_row + jnp.arange(local_rows, dtype=jnp.int32)
    block_ids = row_ids // BLOCK + block_shift
    return jnp.any(block_ids[None, :, None] == structure[:, None, :], axis=2).astype(F32)


def local(root_factor, mid_factor, low_factor, mid_rows, low_parent_rows, low_root_rows, mid_struct, low_struct, low_parent):
    row = lax.axis_index("row")
    lm = lower_part(mid_factor)
    ll = lower_part(low_factor)
    m = jnp.transpose(mid_rows, (0, 2, 1)) * live_mask(512, row * 512, mid_struct, 0)[:, None, :]
    r = jnp.transpose(low_root_rows, (0, 2, 1)) * live_mask(512, row * 512, low_struct, MID // BLOCK)[:, None, :]
    p = jnp.transpose(low_parent_rows, (0, 2, 1)) * live_mask(128, row * 128, low_struct, 0)[:, None, :]
    sigma, m_all, r_all, q_all, lm_all, ll_all = first_step(root_factor, m, r, p, lm, ll)
    mid_cross, low_root, um_c, ul_c, g = second_step(low_parent, sigma, lm, m_all, r_all, q_all, lm_all, ll_all)
    sums = third_step(low_parent, mid_cross, low_root, um_c, ul_c, g, lm, ll)
    mid_diag = jnp.transpose(sums[:128].reshape(2, 64, 128), (0, 2, 1))
    par = sums[128:256].reshape(2, 64, 2, 64)
    low_cross_parent = jnp.transpose(par, (0, 2, 3, 1)).reshape(4, 64, 64)
    low = sums[256:].reshape(2, 32, 2, 64)
    low_diag = jnp.transpose(low, (0, 2, 3, 1)).reshape(4, 64, 32)
    return sigma, mid_diag, mid_cross, low_diag, low_cross_parent, low_root


def solution(mesh):
    rc = P(None, "row", "col")
    in_specs = (P("col", None), P(None, "col", None), P(None, "col", None), rc, rc, rc, P(), P(), P())
    out_specs = (P("row", "col"), rc, rc, rc, rc, rc)
    return jax.shard_map(local, mesh=mesh, in_specs=in_specs, out_specs=out_specs, check_vma=False)
```

profile of v0, /device:TPU:0, one launch (start us, length us, event | category | flops | bytes accessed | tf_op | source)
XLA Modules:
  0.0 291.4 jit_solution(8533614138675237459)
XLA Ops:
  0.7 0.8 compare_reduce_fusion.1
  1.5 0.8 copy.17
  2.3 0.1 compare_reduce_fusion.2
  2.3 0.1 compare_reduce_fusion
  2.5 0.1 iota_compare_fusion.1
  2.6 1.5 multiply_bitcast_fusion.2.p
  4.0 0.1 iota_compare_fusion
  4.2 1.7 broadcast_select_fusion.1.ll
  5.8 1.7 multiply_bitcast_fusion.r
  7.5 1.7 multiply_bitcast_fusion.1.m
  9.2 1.9 broadcast_select_fusion.lm.lm_own
  11.1 148.3 %first_step.1 = (f32[512,256]{1,0:T(8,128)}, f32[2,1024,512]{2,1,0:T(8,128)}, f32[4,512,512]{2,1,0:T(8,128)}, f32[4,512,1024]{2,1,0:T(8,128)}, f32[2,16,64,1024]{3,2,1,0:T(8,128)}, /*index=5*/f32[4,16,32,512]{3,2,1,0:T(8,128)}) custom-call(f32[256,4096]{1,0:T(8,128)} %lr.1, f32[2,64,512]{2,1,0:T(8,128)} %multiply_bitcast_fusion.1.m, ...), custom_call_target="tpu_custom_call" | custom-call | tf_op jit(solution)/shard_map/first_step/pallas_call | solution.py:387
  159.4 72.2 %second_step.1 = (f32[2,128,256]{2,1,0:T(8,128)}, f32[4,64,256]{2,1,0:T(8,128)}, f32[2,1024,256]{2,1,0:T(8,128)}, f32[4,512,256]{2,1,0:T(8,128)}, f32[4,512,64]{2,1,0:T(8,128)}) custom-call(s32[4]{0:T(128)} %parent.3, f32[512,256]{1,0:T(8,128)} %get-tuple-element.38.sigma, f32[2,64,1024]{2,1,0:T(8,128)} %broadcast_select_fusion.lm.lm_own, ...), custom_call_target="tpu_custom_call" | custom-call | tf_op jit(solution)/shard_map/second_step/pallas_call | solution.py:586
  231.6 0.0 copy-start
  231.6 0.0 copy-start.2
  231.6 0.0 copy-start.1
  231.7 53.6 %third_step.1 = f32[320,128]{1,0:T(8,128)} custom-call(s32[4]{0:T(128)} %parent.3, f32[2,128,256]{2,1,0:T(8,128)} %get-tuple-element.40.mid_cross, f32[4,64,256]{2,1,0:T(8,128)} %get-tuple-element.43.low_root, f32[2,1024,256]{2,1,0:T(8,128)} %get-tuple-element.25.um, f32[4,512,256]{2,1,0:T(8,128)} %get-tuple-element.26.ul, ...), custom_call_target="tpu_custom_call" | custom-call | tf_op jit(solution)/shard_map/third_step/pallas_call | solution.py:658
  285.3 0.8 slice.10
  286.0 1.5 fusion.3
  287.5 0.1 reshape.106
  287.6 0.6 copy.19
  288.3 0.1 reshape.108
  288.4 0.8 copy.20
  289.2 0.0 copy-done
  289.2 0.8 copy.24
  290.0 0.0 copy-done.2
  290.0 0.7 copy.25
  290.7 0.0 copy-done.1
  290.7 0.7 copy.26
  (7 shorter events, 0.1 us)
Async XLA Ops:
  231.6 57.6 %copy-start = (f32[512,256]{1,0:T(8,128)S(1)}, f32[512,256]{1,0:T(8,128)}, u32[]{:S(2)}) copy-start(f32[512,256]{1,0:T(8,128)} %get-tuple-element.38.sigma) | copy-start | bytes 1572868
  231.6 58.3 %copy-start.2 = (f32[2,128,256]{2,1,0:T(8,128)S(1)}, f32[2,128,256]{2,1,0:T(8,128)}, u32[]{:S(2)}) copy-start(f32[2,128,256]{2,1,0:T(8,128)} %get-tuple-element.40.mid_cross) | copy-start | bytes 786436
  231.6 59.0 %copy-start.1 = (f32[4,64,256]{2,1,0:T(8,128)S(1)}, f32[4,64,256]{2,1,0:T(8,128)}, u32[]{:S(2)}) copy-start(f32[4,64,256]{2,1,0:T(8,128)} %get-tuple-element.43.low_root) | copy-start | bytes 786436
where the time goes:
time: 294 us; the launch traced here: 291 us
  Pallas kernels  274 us (93%)
  other arithmetic  9.61 us (3%)
  local copies, waits for them, and re-layouts  6.87 us (2%)
    pallas_call x1, Pallas kernels, first_step(): pl.pallas_call(first_kernel, out_shape=(shape(512, 256), shape(MIDS, MID,...  148 us
    pallas_call x1, Pallas kernels, second_step(): pl.pallas_call(second_kernel, out_shape=(shape(MIDS, 128, 256), shape(LOW...  72.2 us
    pallas_call x1, Pallas kernels, third_step(): pl.pallas_call(third_kernel, out_shape=jax.ShapeDtypeStruct((DIAG_ROWS, 1...  53.6 us

commit v1 on v0

v1 whole, which is shorter than its diff:
```python
import functools

import jax
import jax.numpy as jnp
from jax import lax
from jax.experimental import pallas as pl
from jax.experimental.pallas import tpu as pltpu
from jax.sharding import PartitionSpec as P

BLOCK = 256
ROOT = 4096
MID = 1024
LOW = 512
MIDS = 2
LOWS = 4
MESH = pl.DeviceIdType.MESH
F32 = jnp.float32
VMEM = pltpu.VMEM
ANY = pl.ANY


class Net:
    def __init__(self, send_sem, recv_sem):
        self.row = lax.axis_index("row")
        self.col = lax.axis_index("col")
        self.place = {
            "x": lax.div(self.col, 4),
            "z": lax.rem(self.col, 4),
            "y": lax.div(self.row, 2),
            "core": lax.rem(self.row, 2),
        }
        self.send_sem, self.recv_sem, self.used, self.started = send_sem, recv_sem, 0, []

    def at(self, axis, shift):
        if axis == "core":
            return lax.rem(self.place["core"] + shift, 2)
        return lax.rem(self.place[axis] + shift + 4, 4)

    def device(self, **shifts):
        at = {axis: self.at(axis, shifts.get(axis, 0)) for axis in self.place}
        return (at["y"] * 2 + at["core"], at["x"] * 4 + at["z"])

    def greet(self, axes):
        barrier = pltpu.get_barrier_semaphore()
        count = 0
        for axis in axes:
            for shift in (1,) if axis == "core" else (1, -1):
                pl.semaphore_signal(barrier, inc=1, device_id=self.device(**{axis: shift}), device_id_type=MESH)
                count += 1
        pl.semaphore_wait(barrier, count)

    def send(self, src, dst, axis, shift):
        index = self.used
        self.used += 1
        copy = pltpu.make_async_remote_copy(
            src_ref=src,
            dst_ref=dst,
            send_sem=self.send_sem.at[index],
            recv_sem=self.recv_sem.at[index],
            device_id=self.device(**{axis: shift}),
            device_id_type=MESH,
        )
        copy.start()
        self.started.append(copy)
        return copy

    def finish(self):
        for copy in self.started:
            copy.wait_send()


def mult(value, unit):
    return pl.multiple_of(value, unit)


def params(collective_id):
    return pltpu.CompilerParams(collective_id=collective_id, has_side_effects=True, vmem_limit_bytes=62 * 2**20)


class Gather:
    def __init__(self, net, src, dst, whole, half, first, second, local_sem, share=None):
        self.net, self.dst, self.whole, self.half = net, dst, whole, half
        self.first, self.second, self.share = first, second, share
        self.src, self.local_sem, self.sent = src, local_sem, []

    def send(self, *args):
        copy = self.net.send(*args)
        self.sent.append(copy)
        return copy

    def free(self):
        for copy in self.sent:
            copy.wait_send()
        self.net.started = [copy for copy in self.net.started if not any(copy is one for one in self.sent)]

    def spot(self, a, b):
        at = {self.first: self.net.at(self.first, a), self.second: self.net.at(self.second, b)}
        return at["x"], at["z"]

    def piece(self, a, b):
        return self.whole(self.dst, *self.spot(a, b))

    def part(self, a, b, h):
        return self.half(self.dst, *self.spot(a, b), h)

    def start(self):
        net, own = self.net, self.piece(0, 0)
        self.local = pltpu.make_async_copy(self.src, own, self.local_sem)
        self.local.start()
        self.p1 = [self.send(self.src, own, self.first, s) for s in (1, -1)]
        self.p2 = {0: [self.send(self.src, own, self.second, s) for s in (1, -1)]}

    def onward(self, a):
        piece = self.piece(a, 0)
        self.p2[a] = [self.send(piece, piece, self.second, s) for s in (1, -1)]

    def first_ring(self):
        self.fwd = []
        for index, shift in enumerate((1, -1)):
            self.p1[index].wait_recv()
            part = self.part(-shift, 0, index)
            self.fwd.append(self.send(part, part, self.first, shift))
            self.onward(-shift)

    def first_end(self):
        for copy in self.fwd:
            copy.wait_recv()
        self.onward(2)

    def second_ring(self, a):
        copies = []
        for index, shift in enumerate((1, -1)):
            self.p2[a][index].wait_recv()
            part = self.part(a, -shift, index)
            copies.append(self.send(part, part, self.second, shift))
        self.p2[a] = copies

    def second_end(self, a):
        for copy in self.p2[a]:
            copy.wait_recv()

    def finish(self):
        self.local.wait()


class Scatter:
    def __init__(self, net, axis, part, near, far):
        self.net, self.axis, self.part, self.near, self.far = net, axis, part, near, far

    def start(self):
        opposite = self.net.at(self.axis, 2)
        self.first = [
            self.net.send(self.part(opposite, h), self.near[h], self.axis, shift) for h, shift in enumerate((1, -1))
        ]

    def plain(self):
        self.second = [
            self.net.send(self.part(self.net.at(self.axis, shift), 1 - h), self.far[h][1 - h], self.axis, shift)
            for h, shift in enumerate((1, -1))
        ]

    def middle(self):
        for h, shift in enumerate((1, -1)):
            self.first[h].wait_recv()
            self.near[h][...] += self.part(self.net.at(self.axis, shift), h)[...]
            self.second.append(self.net.send(self.near[h], self.far[h][h], self.axis, shift))

    def end(self, out):
        for copy in self.second:
            copy.wait_recv()
        for h in range(2):
            out[h][...] = self.part(self.net.at(self.axis, 0), h)[...] + self.far[0][h][...] + self.far[1][h][...]


class TorusScatter:
    def __init__(self, net, part_xz, part_zx, bufs_xz, bufs_zx):
        self.net, self.bufs = net, (bufs_xz, bufs_zx)
        self.stages = [self.stage(axis, part, bufs[0], bufs[1])
                       for axis, part, bufs in (("x", part_xz, bufs_xz), ("z", part_zx, bufs_zx))]

    def stage(self, axis, part, near, far):
        return Scatter(self.net, axis, part, [near.at[0], near.at[1]], [[far.at[s, h] for h in range(2)] for s in range(2)])

    def start(self):
        for stage in self.stages:
            stage.start()

    def plain(self):
        for stage in self.stages:
            stage.plain()

    def middle(self):
        for stage in self.stages:
            stage.middle()

    def turn(self):
        later = []
        for stage, axis, bufs in zip(self.stages, ("z", "x"), self.bufs):
            sums = bufs[2]
            stage.end([sums.at[0], sums.at[1]])
            part = functools.partial(lambda sums, o, h: sums.at[h, o], sums)
            later.append(self.stage(axis, part, bufs[3], bufs[4]))
            later[-1].start()
            later[-1].plain()
        self.stages = later

    second_middle = middle

    def end(self, out_xz, out_zx):
        for stage, out in zip(self.stages, (out_xz, out_zx)):
            stage.end(out)


def torus_bufs(rows, lanes):
    return [
        VMEM((2, 4, rows, lanes), F32),
        VMEM((2, 2, 4, rows, lanes), F32),
        VMEM((2, 4, rows, lanes), F32),
        VMEM((2, rows, lanes), F32),
        VMEM((2, 2, rows, lanes), F32),
    ]


def split(a):
    high = a.astype(jnp.bfloat16)
    return high, (a - high.astype(F32)).astype(jnp.bfloat16)


def dot3(a, b):
    go = functools.partial(jnp.dot, preferred_element_type=F32)
    return go(a[0], b[0]) + (go(a[0], b[1]) + go(a[1], b[0]))


class Ring:
    def __init__(self, net, pieces, halves, share=True):
        self.net, self.pieces, self.halves, self.share = net, pieces, halves, share

    def pair_up(self, place):
        if self.share:
            self.pair += [self.net.send(part, part, "core", 1) for part in self.pieces(place)]

    def start(self):
        own = self.pieces(self.net.at("y", 0))
        self.near = [[self.net.send(part, part, "y", s) for part in own] for s in (1, -1)]
        self.pair = []
        self.pair_up(self.net.at("y", 0))

    def middle(self):
        self.far = []
        for index, shift in enumerate((1, -1)):
            for copy in self.near[index]:
                copy.wait_recv()
            place = self.net.at("y", -shift)
            self.far += [self.net.send(part, part, "y", shift) for part in self.halves(place, index)]
            self.pair_up(place)

    def end(self):
        for copy in self.far:
            copy.wait_recv()
        self.pair_up(self.net.at("y", 2))

    def finish(self):
        for copy in self.pair:
            copy.wait_recv()


CHUNKS = 4
STEP = 256


class Spread:
    def __init__(self, net, source, out, send_sem, recv_sem, local_sem):
        self.net, self.source, self.out = net, source, out
        self.send_sem, self.recv_sem, self.local_sem = send_sem, recv_sem, local_sem
        x, z = net.place["x"], net.place["z"]
        self.lanes = pl.ds(mult(lax.rem(z, 2) * 256, 256), 256)
        self.away = lax.rem(net.place["y"] - x + 4, 4)
        self.is_core = net.place["core"] == lax.div(z, 2)

    def spot(self, ref, way, chunk, lanes):
        per = ref.shape[1] // STEP
        return ref.at[way * (ref.shape[0] // 2) + chunk // per, pl.ds(chunk % per * STEP, STEP), lanes]

    def copy(self, way, chunk, pair):
        place = self.spot(self.out, way, chunk, slice(None))
        index = pair * 2 * CHUNKS + way * CHUNKS + chunk
        to = {"core": 1} if pair else {"y": 1 - 2 * way}
        return pltpu.make_async_remote_copy(
            src_ref=place, dst_ref=place,
            send_sem=self.send_sem.at[index], recv_sem=self.recv_sem.at[index],
            device_id=self.net.device(**to), device_id_type=MESH,
        )

    def load(self):
        return pltpu.make_async_copy(self.source.at[:, :, self.lanes], self.out, self.local_sem)

    def start(self):
        @pl.when(jnp.logical_and(self.is_core, self.away == 0))
        def _():
            self.load().start()
            self.load().wait()
            for pair in range(2):
                for chunk in range(CHUNKS):
                    for way in range(2):
                        self.copy(way, chunk, pair).start()

    def onward(self, first, last):
        for away in (1, 2, 3):
            @pl.when(jnp.logical_and(self.is_core, self.away == away))
            def _():
                for step in range(first, last):
                    for way in range(2):
                        hops = away if way == 0 else 4 - away
                        chunk = step + 1 - hops
                        if 0 <= chunk < CHUNKS:
                            self.copy(way, chunk, 0).wait_recv()
                            if hops < 3:
                                self.copy(way, chunk, 0).start()
                            self.copy(way, chunk, 1).start()

    def finish(self):
        for chunk in range(CHUNKS):
            for way in range(2):
                @pl.when(jnp.logical_and(self.is_core, self.away != (3, 1)[way]))
                def _():
                    self.copy(way, chunk, 0).wait_send()

                @pl.when(self.is_core)
                def _():
                    self.copy(way, chunk, 1).wait_send()

                @pl.when(jnp.logical_not(self.is_core))
                def _():
                    self.copy(way, chunk, 1).wait_recv()


def dot3_nt(a, b):
    go = lambda s, t: lax.dot_general(s, t, (((1,), (1,)), ((), ())), preferred_element_type=F32)
    return go(a[0], b[0]) + (go(a[0], b[1]) + go(a[1], b[0]))


def main_kernel(parent, lr, lm_own, m, r, p, ll, sigma, out_m, out_l, g, um_c, ul_c, lm_all, p_all,
                m_all, r_all, p_mine, g_in, ll_all, stage, high, low, s_high, s_low, terms, cm, cl,
                acc_m, acc_l, core_m, core_l, near_m, near_l, far_m, far_l, *scratch):
    bufs_xz, bufs_zx, (send_sem, recv_sem, spread_send, spread_recv, local_sem, load_sem) = (
        scratch[:5], scratch[5:10], scratch[10:]
    )
    net = Net(send_sem, recv_sem)
    core, y = net.place["core"], net.place["y"]
    other = 1 - core

    def band(block):
        return pl.ds(block * 256, 256)

    def root_block(b):
        return cm.at[b // 4, band(b % 4), :] if b < 8 else cl.at[(b - 8) // 2, band(b % 2), :]

    root_loads = [
        pltpu.make_async_copy(
            lr.at[pl.ds(128 * t, 128), pl.ds(mult(net.row * 512 + 256 * h, 256), 256)], acc_m.at[h, t], load_sem.at[2 * h + t]
        )
        for h in range(2)
        for t in range(2)
    ]
    root_loads += [pltpu.make_async_copy(lr.at[:, band(b)], root_block(b), load_sem.at[4 + b]) for b in range(16)]
    for load in root_loads:
        load.start()
    net.greet(("x", "z", "y", "core"))

    def rows(x, z, n):
        return pl.ds(mult((x * 4 + z) * n, n), n)

    def eighth(n):
        return pl.ds(mult(y * n, n), n)

    two = pl.ds(2 * core, 2)
    def p_lanes(o):
        return pl.ds(mult(o * 256, 256), 256)

    ring_p = Ring(net, lambda o: [p_mine.at[:, :, p_lanes(o)]], lambda o, h: [p_mine.at[h, :, p_lanes(o)]], share=False)
    ga_ps = tuple(
        Gather(
            net, p_mine.at[h], p_all,
            lambda ref, x, z, h=h: ref.at[2 * core + h, rows(x, z, 32), :],
            lambda ref, x, z, part, h=h: ref.at[2 * core + h, pl.ds(mult((x * 4 + z) * 32 + 16 * part, 16), 16), :],
            first, second, local_sem.at[(0, 5)[h]],
        )
        for h, (first, second) in enumerate((("x", "z"), ("z", "x")))
    )
    ga_ll = Gather(
        net, ll.at[two, eighth(8), :], ll_all,
        lambda ref, x, z: ref.at[two, x * 4 + z, eighth(8), :],
        lambda ref, x, z, h: ref.at[2 * core + h, x * 4 + z, eighth(8), :],
        "z", "x", local_sem.at[1],
    )
    ga_lm = Gather(
        net, lm_own.at[core, eighth(16), :], lm_all,
        lambda ref, x, z: ref.at[core, x * 4 + z, eighth(16), :],
        lambda ref, x, z, h: ref.at[core, x * 4 + z, pl.ds(mult(y * 16 + 8 * h, 8), 8), :],
        "x", "z", local_sem.at[2],
    )
    ga_m = Gather(
        net, m, m_all,
        lambda ref, x, z: ref.at[:, rows(x, z, 64), :],
        lambda ref, x, z, h: ref.at[h, rows(x, z, 64), :],
        "x", "z", local_sem.at[3],
    )
    ga_r = Gather(
        net, r, r_all,
        lambda ref, x, z: ref.at[:, rows(x, z, 32), :],
        lambda ref, x, z, h: ref.at[pl.ds(2 * h, 2), rows(x, z, 32), :],
        "z", "x", local_sem.at[4],
    )
    def ll_parts(o):
        return [ll_all.at[two, pl.ds(8 * g, 8), pl.ds(mult(o * 8, 8), 8), pl.ds(0, 256 * (g + 1))] for g in range(2)]

    def lm_parts(o):
        return [
            lm_all.at[core, pl.ds(4 * g, 4), pl.ds(mult(o * 16, 16), 16), pl.ds(0, 256 * (g + 1))] for g in range(4)
        ]

    ring_ll = Ring(net, ll_parts, lambda o, h: ll_parts(o)[1:] if h else ll_parts(o)[:1])
    ring_lm = Ring(net, lm_parts, lambda o, h: lm_parts(o)[:3] if h else lm_parts(o)[3:])

    mine = pl.ds(mult(net.row * 128, 128), 128)
    local_p = pltpu.make_async_copy(p.at[two], p_mine.at[:, :, mine], local_sem.at[5])
    local_p.start()
    pair_p = net.send(p.at[pl.ds(2 * other, 2)], p_mine.at[:, :, mine], "core", 1)
    small, large = (ga_ll, ga_lm), (ga_m, ga_r)
    for item in small + large:
        item.start()
    local_p.wait()
    pair_p.wait_recv()
    ring_p.start()

    base = net.col * 256

    def lower(block, first):
        at = lambda axis: lax.broadcasted_iota(jnp.int32, (256, 256), axis)
        return jnp.where(first + at(1) <= base + at(0), block, 0.0)

    for load in root_loads:
        load.wait()
    for h in range(2):
        block = lower(acc_m[h].reshape(256, 256), net.row * 512 + 256 * h)
        high[0, band(h), :256], low[0, band(h), :256] = split(jnp.transpose(block))
    left = lambda: (high[0, :512, :256], low[0, :512, :256])

    def root_terms(first, last):
        @pl.loop(first, last)
        def _(b):
            block = lower(cm[lax.div(b, 4), pl.ds(mult(lax.rem(b, 4) * 256, 256), 256), :], b * 256)
            terms[lax.div(b, 4), lax.rem(b, 4)] = dot3(left(), split(block))
            block = lower(cl[lax.div(b, 2), pl.ds(mult(lax.rem(b, 2) * 256, 256), 256), :], b * 256 + 2048)
            terms[2 + lax.div(b, 4), lax.rem(b, 4)] = dot3(left(), split(block))

    sc = TorusScatter(
        net,
        lambda o, h: terms.at[o, :, pl.ds(128 * h, 128), :],
        lambda o, h: terms.at[:, o, pl.ds(256 + 128 * h, 128), :],
        bufs_xz, bufs_zx,
    )
    ring_p.middle()
    root_terms(0, 2)
    ring_p.end()
    for item in ga_ps:
        item.start()
    for item in small:
        item.first_ring()
    root_terms(2, 4)
    for item in small:
        item.first_end()
    for item in large:
        item.first_ring()
    root_terms(4, 6)
    for a in (0, -1, 1, 2):
        for item in small:
            item.second_ring(a)
    root_terms(6, 8)
    for item in large:
        item.first_end()
    for item in small:
        for a in (0, -1, 1, 2):
            item.second_end(a)
        item.finish()
    ring_ll.start()
    ring_lm.start()
    sc.start()
    for item in ga_ps:
        item.first_ring()
    for item in large:
        item.second_ring(0)
    for item in ga_ps:
        item.first_end()
    ring_ll.middle()
    ring_lm.middle()
    for a in (-1, 1):
        for item in large:
            item.second_ring(a)
    for a in (0, -1, 1):
        for item in ga_ps:
            item.second_ring(a)
    sc.plain()
    for item in large + ga_ps:
        item.second_ring(2)
    ring_ll.end()
    ring_lm.end()
    sc.middle()
    ring_lm.finish()
    lm_loads = [pltpu.make_async_copy(lm_all.at[k], stage.at[k], load_sem.at[k]) for k in range(MIDS)]
    for load in lm_loads:
        load.start()
    for item in large + ga_ps:
        for a in (0, -1, 1, 2):
            item.second_end(a)
        item.finish()
    shared_p = []
    for o in range(4):
        part = p_all.at[two, pl.ds(128 * o, 128), :]
        shared_p.append(net.send(part, part, "core", 1))
    spread_m = Spread(net, m_all, um_c, spread_send.at[0], spread_recv.at[0], local_sem.at[6])
    spread_l = Spread(net, r_all, ul_c, spread_send.at[1], spread_recv.at[1], local_sem.at[7])
    spread_m.start()
    spread_l.start()

    def mid_nodes(lanes):
        for load in lm_loads:
            load.wait()

        @pl.loop(0, MIDS)
        def _(k):
            for j in range(4):
                total = None
                for t in range(j, 4):
                    tile = jnp.transpose(stage[k, pl.ds(4 * t, 4), :, band(j)].reshape(256, 256))
                    term = dot3(split(tile), split(m_all[k, band(t), lanes]))
                    total = term if total is None else total + term
                m_all[k, band(j), lanes] = total
                high[k, band(j), lanes], low[k, band(j), lanes] = split(total)

    ga_m.free()
    mid_nodes(pl.ds(0, 512))
    sc.turn()
    ring_ll.finish()
    for copy in shared_p:
        copy.wait_recv()
    p_loads = [
        pltpu.make_async_copy(p_all.at[i, pl.ds(64 * t, 64), :], stage.at[i // 2, i % 2 * 8 + t], load_sem.at[8 * i + t])
        for i in range(LOWS)
        for t in range(8)
    ]
    for load in p_loads:
        load.start()

    def low_nodes(first, lanes, with_g):
        for load in p_loads[8 * first : 8 * first + 16]:
            load.wait()

        @pl.loop(first, first + 2)
        def _(i):
            k = parent[i]
            own = split(lm_own[k]) if with_g else None
            for t in range(2):
                p_both = split(stage[first // 2, pl.ds((i - first) * 8 + 4 * t, 4), :, :].reshape(256, MID))
                r_all[i, band(t), lanes] -= dot3(p_both, (high[k, :, lanes], low[k, :, lanes]))
                if with_g:
                    g_in[band(t), :] = dot3_nt(p_both, own)
            for j in range(2):
                total, g_total = None, None
                for t in range(j, 2):
                    tile = split(jnp.transpose(ll_all[i, pl.ds(8 * t, 8), :, band(j)].reshape(256, 256)))
                    term = dot3(tile, split(r_all[i, band(t), lanes]))
                    total = term if total is None else total + term
                    if with_g:
                        term = dot3(tile, split(g_in[band(t), :]))
                        g_total = term if g_total is None else g_total + term
                r_all[i, band(j), lanes] = total
                if with_g:
                    g[i, band(j), :] = g_total

    both_onward = lambda first, last: (spread_m.onward(first, last), spread_l.onward(first, last))
    ga_r.free()
    low_nodes(0, pl.ds(0, 512), True)
    sc.second_middle()
    both_onward(0, 2)
    low_nodes(2, pl.ds(0, 512), True)
    both_onward(2, 4)
    for load in lm_loads:
        load.start()
    outs = lambda first: [sigma.at[pl.ds(first + 128 * h, 128), :] for h in range(2)]
    sc.end(outs(0), outs(256))
    s_high[...], s_low[...] = split(sigma[...])

    def slab(ref, unit, d, k):
        return ref.at[:, pl.ds(mult((2 * net.at("y", d) + k) * unit, unit), unit), :]

    def multiply(d, k):
        both = (slab(high, 128, d, k)[...].reshape(256, 512), slab(low, 128, d, k)[...].reshape(256, 512))
        slab(cm, 128, d, k)[...] = -dot3(both, (s_high[...], s_low[...])).reshape(MIDS, 128, 256)
        both = split(slab(r_all, 64, d, k)[...].reshape(256, 512))
        slab(cl, 64, d, k)[...] = -dot3(both, (s_high[...], s_low[...])).reshape(LOWS, 64, 256)

    order = (2, 1, -1, 0)
    pairs = {}
    for d in order:
        multiply(d, other)
        pairs[d] = [
            net.send(slab(cm, 128, d, other), core_m.at[d % 4], "core", 1),
            net.send(slab(cl, 64, d, other), core_l.at[d % 4], "core", 1),
        ]
    firsts = []
    for d in order:
        if d == -1:
            both_onward(4, CHUNKS + 2)
        multiply(d, core)
        for copy in pairs[d]:
            copy.wait_recv()
        acc_m[d % 4] = core_m[d % 4] + slab(cm, 128, d, core)[...]
        acc_l[d % 4] = core_l[d % 4] + slab(cl, 64, d, core)[...]
        if d == 2:
            firsts = [net.send(acc_m.at[2], near_m, "y", 1), net.send(acc_l.at[2], near_l, "y", -1)]
    seconds = [net.send(acc_l.at[1], far_l.at[0], "y", 1), net.send(acc_m.at[3], far_m.at[1], "y", -1)]

    block_column = pl.ds(0, 256)
    spread_m.finish()
    spread_l.finish()
    column_loads = [
        pltpu.make_async_copy(src, dst.at[:, :, block_column], local_sem.at[index])
        for index, (src, dst) in enumerate(((um_c, m_all), (ul_c, r_all)))
    ]
    for load in column_loads:
        load.start()
    for load in column_loads:
        load.wait()
    mid_nodes(block_column)
    for load in p_loads:
        load.start()
    column_out = [
        pltpu.make_async_copy(src.at[:, :, block_column], dst, local_sem.at[index])
        for index, (dst, src) in enumerate(((um_c, m_all), (ul_c, r_all)))
    ]
    column_out[0].start()
    firsts[0].wait_recv()
    near_m[...] += acc_m[1]
    seconds.append(net.send(near_m, far_m.at[0], "y", 1))
    firsts[1].wait_recv()
    near_l[...] += acc_l[3]
    seconds.append(net.send(near_l, far_l.at[1], "y", -1))
    low_nodes(0, block_column, False)
    low_nodes(2, block_column, False)
    column_out[1].start()
    for copy in seconds:
        copy.wait_recv()
    out_m[...] = acc_m[0] + far_m[0] + far_m[1]
    out_l[...] = acc_l[0] + far_l[0] + far_l[1]
    for copy in column_out:
        copy.wait()
    net.finish()


SEMS = 240


def main_step(*arrays):
    shape = lambda *dims: jax.ShapeDtypeStruct(dims, F32)
    vmem, hbm = pl.BlockSpec(memory_space=VMEM), pl.BlockSpec(memory_space=ANY)
    block = lambda *dims: VMEM(dims, F32)
    half = lambda *dims: VMEM(dims, jnp.bfloat16)
    return pl.pallas_call(
        main_kernel,
        out_shape=(
            shape(512, 256), shape(MIDS, 128, 256), shape(LOWS, 64, 256), shape(LOWS, LOW, 64),
            shape(MIDS, MID, 256), shape(LOWS, LOW, 256), shape(MIDS, 16, 64, MID), shape(LOWS, LOW, MID),
        ),
        in_specs=[pl.BlockSpec(memory_space=pltpu.SMEM), hbm, vmem] + [hbm] * 4,
        out_specs=[vmem] * 4 + [hbm] * 4,
        scratch_shapes=[
            block(MIDS, MID, 512), block(LOWS, LOW, 512), block(2, 32, MID), block(LOW, 64),
            block(LOWS, 16, 32, LOW), block(MIDS, 16, 64, MID), half(MIDS, MID, 512), half(MIDS, MID, 512),
            half(512, 256), half(512, 256), block(4, 4, 512, 256), block(MIDS, MID, 256), block(LOWS, LOW, 256),
            block(4, MIDS, 128, 256), block(4, LOWS, 64, 256), block(4, MIDS, 128, 256), block(4, LOWS, 64, 256),
            block(MIDS, 128, 256), block(LOWS, 64, 256), block(2, MIDS, 128, 256), block(2, LOWS, 64, 256),
        ] + torus_bufs(128, 256) + torus_bufs(128, 256) + [
            pltpu.SemaphoreType.DMA((SEMS,)),
            pltpu.SemaphoreType.DMA((SEMS,)),
            pltpu.SemaphoreType.DMA((2, 4 * CHUNKS)),
            pltpu.SemaphoreType.DMA((2, 4 * CHUNKS)),
            pltpu.SemaphoreType.DMA((8,)),
            pltpu.SemaphoreType.DMA((32,)),
        ],
        compiler_params=params(0),
        name="main_step",
    )(*arrays)


DIAG_ROWS = 320


def third_kernel(parent, mid_cross, low_root, um, ul, g, lm, ll, out, terms, lm_t, ll_t, *scratch):
    bufs_xz, bufs_zx, (send_sem, recv_sem) = scratch[:5], scratch[5:10], scratch[10:]
    net = Net(send_sem, recv_sem)
    net.greet(("x", "z"))
    for p in range(MIDS):
        lm_t[p] = jnp.transpose(lm[p])
    for i in range(LOWS):
        ll_t[i] = jnp.transpose(ll[i])
    low_rows = pl.ds(mult(net.row * 64, 64), 64)
    for p in range(MIDS):
        mine = split(lm_t[p, pl.ds(mult(net.row * 128, 128), 128), :])
        term = dot3_nt(split(lm_t[p]), mine) - dot3_nt(split(um[p]), split(mid_cross[p]))
        terms[:, :, pl.ds(64 * p, 64), :] = term.reshape(4, 4, 64, 128)
    for pair in range(2):
        par, own = [], []
        for i in (2 * pair, 2 * pair + 1):
            p = parent[i]
            root, g_mine = split(low_root[i]), split(g[i, low_rows, :])
            par.append(-(dot3_nt(split(um[p]), root) + dot3_nt(split(lm_t[p]), g_mine)))
            own.append(
                dot3_nt(split(ll_t[i]), split(ll_t[i, low_rows, :])) + dot3_nt(split(g[i]), g_mine)
                - dot3_nt(split(ul[i]), root)
            )
        terms[:, :, pl.ds(128 + 64 * pair, 64), :] = jnp.concatenate(par, axis=1).reshape(4, 4, 64, 128)
        terms[:, :, pl.ds(256 + 32 * pair, 32), :] = jnp.concatenate(own, axis=1).reshape(4, 4, 32, 128)
    half = DIAG_ROWS // 4

    def outs(base):
        return [out.at[pl.ds(base + half * h, half), :] for h in range(2)]

    sc = TorusScatter(
        net,
        lambda o, h: terms.at[o, :, pl.ds(half * h, half), :],
        lambda o, h: terms.at[:, o, pl.ds(2 * half + half * h, half), :],
        bufs_xz, bufs_zx,
    )
    sc.start()
    sc.plain()
    sc.middle()
    sc.turn()
    sc.second_middle()
    sc.end(outs(0), outs(2 * half))
    net.finish()


def third_step(parent, *arrays):
    return pl.pallas_call(
        third_kernel,
        out_shape=jax.ShapeDtypeStruct((DIAG_ROWS, 128), F32),
        in_specs=[pl.BlockSpec(memory_space=pltpu.SMEM)] + [pl.BlockSpec(memory_space=VMEM)] * 7,
        out_specs=pl.BlockSpec(memory_space=VMEM),
        scratch_shapes=[
            VMEM((4, 4, DIAG_ROWS, 128), F32), VMEM((MIDS, MID, 64), F32), VMEM((LOWS, LOW, 32), F32),
        ] + torus_bufs(DIAG_ROWS // 4, 128) + torus_bufs(DIAG_ROWS // 4, 128) + [
            pltpu.SemaphoreType.DMA((32,)),
            pltpu.SemaphoreType.DMA((32,)),
        ],
        compiler_params=params(1),
        name="third_step",
    )(parent, *arrays)


def lower_part(factor):
    rows_here = factor.shape[1]
    row_ids = lax.axis_index("col") * rows_here + lax.broadcasted_iota(jnp.int32, factor.shape[1:], 0)
    col_ids = lax.broadcasted_iota(jnp.int32, factor.shape[1:], 1)
    return jnp.where((col_ids <= row_ids)[None], factor, 0.0)


def live_mask(local_rows, first_row, structure, block_shift):
    row_ids = first_row + jnp.arange(local_rows, dtype=jnp.int32)
    block_ids = row_ids // BLOCK + block_shift
    return jnp.any(block_ids[None, :, None] == structure[:, None, :], axis=2).astype(F32)


def local(root_factor, mid_factor, low_factor, mid_rows, low_parent_rows, low_root_rows, mid_struct, low_struct, low_parent):
    row = lax.axis_index("row")
    lm = lower_part(mid_factor)
    ll = lower_part(low_factor)
    m = jnp.transpose(mid_rows, (0, 2, 1)) * live_mask(512, row * 512, mid_struct, 0)[:, None, :]
    r = jnp.transpose(low_root_rows, (0, 2, 1)) * live_mask(512, row * 512, low_struct, MID // BLOCK)[:, None, :]
    p = jnp.transpose(low_parent_rows, (0, 2, 1)) * live_mask(128, row * 128, low_struct, 0)[:, None, :]
    sigma, mid_cross, low_root, g, um_c, ul_c, _, _ = main_step(low_parent, root_factor, lm, m, r, p, ll)
    sums = third_step(low_parent, mid_cross, low_root, um_c, ul_c, g, lm, ll)
    mid_diag = jnp.transpose(sums[:128].reshape(2, 64, 128), (0, 2, 1))
    par = sums[128:256].reshape(2, 64, 2, 64)
    low_cross_parent = jnp.transpose(par, (0, 2, 3, 1)).reshape(4, 64, 64)
    low = sums[256:].reshape(2, 32, 2, 64)
    low_diag = jnp.transpose(low, (0, 2, 3, 1)).reshape(4, 64, 32)
    return sigma, mid_diag, mid_cross, low_diag, low_cross_parent, low_root


def solution(mesh):
    rc = P(None, "row", "col")
    in_specs = (P("col", None), P(None, "col", None), P(None, "col", None), rc, rc, rc, P(), P(), P())
    out_specs = (P("row", "col"), rc, rc, rc, rc, rc)
    return jax.shard_map(local, mesh=mesh, in_specs=in_specs, out_specs=out_specs, check_vma=False)
```

time: 294 us -> 257 us (0.87)
  Pallas kernels: 274 us -> 238 us
    pallas_call x1, Pallas kernels: 53.6 us -> 33.4 us  [third_step(): pl.pallas_call(third_kernel, out_shape=jax.ShapeDtypeStruct((DIAG_ROWS, 1...]
    pallas_call x2 -> x1, Pallas kernels: 221 us -> 205 us  [main_step(): pl.pallas_call(main_kernel, out_shape=(shape(512, 256), shape(MIDS, 128,...]
where the time goes in v1:
time: 257 us; the launch traced here: 255 us
  Pallas kernels  238 us (93%)
  other arithmetic  9.62 us (4%)
  local copies, waits for them, and re-layouts  6.87 us (3%)
    pallas_call x1, Pallas kernels, main_step(): pl.pallas_call(main_kernel, out_shape=(shape(512, 256), shape(MIDS, 128,...  205 us
    pallas_call x1, Pallas kernels, third_step(): pl.pallas_call(third_kernel, out_shape=jax.ShapeDtypeStruct((DIAG_ROWS, 1...  33.4 us

profile of v1, /device:TPU:0, one launch (start us, length us, event | category | flops | bytes accessed | tf_op | source)
XLA Modules:
  0.0 255.3 jit_solution(15837821599664179590)
XLA Ops:
  0.7 0.8 compare_reduce_fusion.1
  1.5 0.8 copy.17
  2.3 0.1 compare_reduce_fusion.2
  2.3 0.1 compare_reduce_fusion
  2.5 0.1 iota_compare_fusion.1
  2.6 1.5 multiply_bitcast_fusion.2.p
  4.0 0.1 iota_compare_fusion
  4.2 1.7 broadcast_select_fusion.1.ll
  5.8 1.7 multiply_bitcast_fusion.r
  7.5 1.7 multiply_bitcast_fusion.1.m
  9.2 1.9 broadcast_select_fusion.lm_own.lm
  11.1 204.7 %main_step.1 = (f32[512,256]{1,0:T(8,128)}, f32[2,128,256]{2,1,0:T(8,128)}, f32[4,64,256]{2,1,0:T(8,128)}, f32[4,512,64]{2,1,0:T(8,128)}, f32[2,1024,256]{2,1,0:...) custom-call(s32[4]{0:T(128)} %parent.3, f32[256,4096]{1,0:T(8,128)} %lr.1, ...), custom_call_target="tpu_custom_call" | custom-call | tf_op jit(solution)/shard_map/main_step/pallas_call | solution.py:669
  215.8 0.0 copy-start.2
  215.8 0.0 copy-start.1
  215.8 0.0 copy-start
  215.8 33.4 %third_step.1 = f32[320,128]{1,0:T(8,128)} custom-call(s32[4]{0:T(128)} %parent.3, f32[2,128,256]{2,1,0:T(8,128)} %get-tuple-element.30.mid_cross, f32[4,64,256]{2,1,0:T(8,128)} %get-tuple-element.33.low_root, f32[2,1024,256]{2,1,0:T(8,128)} %get-tuple-element.15.um, f32[4,512,256]{2,1,0:T(8,128)} %get-tuple-element.16.ul, ...), custom_call_target="tpu_custom_call" | custom-call | tf_op jit(solution)/shard_map/third_step/pallas_call | solution.py:745
  249.2 0.8 slice.10
  250.0 1.5 fusion.3
  251.5 0.1 reshape.106
  251.6 0.6 copy.19
  252.2 0.1 reshape.108
  252.4 0.8 copy.20
  253.1 0.0 copy-done.2
  253.1 0.8 copy.24
  253.9 0.0 copy-done.1
  253.9 0.7 copy.25
  254.6 0.0 copy-done
  254.6 0.7 copy.26
  (7 shorter events, 0.1 us)
Async XLA Ops:
  215.8 37.4 %copy-start.2 = (f32[512,256]{1,0:T(8,128)S(1)}, f32[512,256]{1,0:T(8,128)}, u32[]{:S(2)}) copy-start(f32[512,256]{1,0:T(8,128)} %get-tuple-element.28) | copy-start | bytes 1572868
  215.8 38.1 %copy-start.1 = (f32[2,128,256]{2,1,0:T(8,128)S(1)}, f32[2,128,256]{2,1,0:T(8,128)}, u32[]{:S(2)}) copy-start(f32[2,128,256]{2,1,0:T(8,128)} %get-tuple-element.30.mid_cross) | copy-start | bytes 786436
  215.8 38.8 %copy-start = (f32[4,64,256]{2,1,0:T(8,128)S(1)}, f32[4,64,256]{2,1,0:T(8,128)}, u32[]{:S(2)}) copy-start(f32[4,64,256]{2,1,0:T(8,128)} %get-tuple-element.33.low_root) | copy-start | bytes 786436

commit v2 on v1

--- a/solution.py
+++ b/solution.py
@@ -485,7 +485,6 @@
         item.finish()
     ring_ll.start()
     ring_lm.start()
-    sc.start()
     for item in ga_ps:
         item.first_ring()
     for item in large:
@@ -500,12 +499,12 @@
     for a in (0, -1, 1):
         for item in ga_ps:
             item.second_ring(a)
-    sc.plain()
     for item in large + ga_ps:
         item.second_ring(2)
+    sc.start()
+    sc.plain()
     ring_ll.end()
     ring_lm.end()
-    sc.middle()
     ring_lm.finish()
     lm_loads = [pltpu.make_async_copy(lm_all.at[k], stage.at[k], load_sem.at[k]) for k in range(MIDS)]
     for load in lm_loads:
@@ -540,7 +539,7 @@
 
     ga_m.free()
     mid_nodes(pl.ds(0, 512))
-    sc.turn()
+    sc.middle()
     ring_ll.finish()
     for copy in shared_p:
         copy.wait_recv()
@@ -580,11 +579,13 @@
 
     both_onward = lambda first, last: (spread_m.onward(first, last), spread_l.onward(first, last))
     ga_r.free()
+    both_onward(0, 1)
     low_nodes(0, pl.ds(0, 512), True)
+    sc.turn()
+    both_onward(1, 3)
     sc.second_middle()
-    both_onward(0, 2)
     low_nodes(2, pl.ds(0, 512), True)
-    both_onward(2, 4)
+    both_onward(3, 5)
     for load in lm_loads:
         load.start()
     outs = lambda first: [sigma.at[pl.ds(first + 128 * h, 128), :] for h in range(2)]
@@ -611,7 +612,7 @@
     firsts = []
     for d in order:
         if d == -1:
-            both_onward(4, CHUNKS + 2)
+            both_onward(5, CHUNKS + 2)
         multiply(d, core)
         for copy in pairs[d]:
             copy.wait_recv()

time: 257 us -> 240 us (0.934)
  Pallas kernels: 238 us -> 221 us
    pallas_call x1, Pallas kernels: 205 us -> 187 us  [main_step(): pl.pallas_call(main_kernel, out_shape=(shape(512, 256), shape(MIDS, 128,...]
where the time goes in v2:
time: 240 us; the launch traced here: 239 us
  Pallas kernels  221 us (92%)
  other arithmetic  9.62 us (4%)
  local copies, waits for them, and re-layouts  6.87 us (3%)
    pallas_call x1, Pallas kernels, main_step(): pl.pallas_call(main_kernel, out_shape=(shape(512, 256), shape(MIDS, 128,...  187 us
    pallas_call x1, Pallas kernels, third_step(): pl.pallas_call(third_kernel, out_shape=jax.ShapeDtypeStruct((DIAG_ROWS, 1...  34.6 us

profile of v2, /device:TPU:0, one launch (start us, length us, event | category | flops | bytes accessed | tf_op | source)
XLA Modules:
  0.0 238.8 jit_solution(6326350251525953708)
XLA Ops:
  0.7 0.8 compare_reduce_fusion.1
  1.5 0.8 copy.17
  2.3 0.1 compare_reduce_fusion.2
  2.3 0.1 compare_reduce_fusion
  2.5 0.1 iota_compare_fusion.1
  2.6 1.5 multiply_bitcast_fusion.2.p
  4.0 0.1 iota_compare_fusion
  4.2 1.7 broadcast_select_fusion.1.ll
  5.8 1.7 multiply_bitcast_fusion.r
  7.5 1.7 multiply_bitcast_fusion.1.m
  9.2 1.9 broadcast_select_fusion.lm_own.lm
  11.1 186.9 %main_step.1 = (f32[512,256]{1,0:T(8,128)}, f32[2,128,256]{2,1,0:T(8,128)}, f32[4,64,256]{2,1,0:T(8,128)}, f32[4,512,64]{2,1,0:T(8,128)}, f32[2,1024,256]{2,1,0:...) custom-call(s32[4]{0:T(128)} %parent.3, f32[256,4096]{1,0:T(8,128)} %lr.1, ...), custom_call_target="tpu_custom_call" | custom-call | tf_op jit(solution)/shard_map/main_step/pallas_call | solution.py:670
  198.0 0.0 copy-start.2
  198.0 0.0 copy-start.1
  198.0 0.0 copy-start
  198.0 34.6 %third_step.1 = f32[320,128]{1,0:T(8,128)} custom-call(s32[4]{0:T(128)} %parent.3, f32[2,128,256]{2,1,0:T(8,128)} %get-tuple-element.30.mid_cross, f32[4,64,256]{2,1,0:T(8,128)} %get-tuple-element.33.low_root, f32[2,1024,256]{2,1,0:T(8,128)} %get-tuple-element.15.um, f32[4,512,256]{2,1,0:T(8,128)} %get-tuple-element.16.ul, ...), custom_call_target="tpu_custom_call" | custom-call | tf_op jit(solution)/shard_map/third_step/pallas_call | solution.py:746
  232.6 0.8 slice.10
  233.4 1.5 fusion.3
  234.9 0.1 reshape.106
  235.0 0.6 copy.19
  235.7 0.1 reshape.108
  235.8 0.8 copy.20
  236.6 0.0 copy-done.2
  236.6 0.8 copy.24
  237.3 0.0 copy-done.1
  237.3 0.7 copy.25
  238.1 0.0 copy-done
  238.1 0.7 copy.26
  (7 shorter events, 0.1 us)
Async XLA Ops:
  198.0 38.5 %copy-start.2 = (f32[512,256]{1,0:T(8,128)S(1)}, f32[512,256]{1,0:T(8,128)}, u32[]{:S(2)}) copy-start(f32[512,256]{1,0:T(8,128)} %get-tuple-element.28) | copy-start | bytes 1572868
  198.0 39.3 %copy-start.1 = (f32[2,128,256]{2,1,0:T(8,128)S(1)}, f32[2,128,256]{2,1,0:T(8,128)}, u32[]{:S(2)}) copy-start(f32[2,128,256]{2,1,0:T(8,128)} %get-tuple-element.30.mid_cross) | copy-start | bytes 786436
  198.0 40.0 %copy-start = (f32[4,64,256]{2,1,0:T(8,128)S(1)}, f32[4,64,256]{2,1,0:T(8,128)}, u32[]{:S(2)}) copy-start(f32[4,64,256]{2,1,0:T(8,128)} %get-tuple-element.33.low_root) | copy-start | bytes 786436

commit v3 on v2

--- a/solution.py
+++ b/solution.py
@@ -40,14 +40,18 @@
         at = {axis: self.at(axis, shifts.get(axis, 0)) for axis in self.place}
         return (at["y"] * 2 + at["core"], at["x"] * 4 + at["z"])
 
-    def greet(self, axes):
+    def greet(self, axes, wait=True):
         barrier = pltpu.get_barrier_semaphore()
         count = 0
         for axis in axes:
             for shift in (1,) if axis == "core" else (1, -1):
                 pl.semaphore_signal(barrier, inc=1, device_id=self.device(**{axis: shift}), device_id_type=MESH)
                 count += 1
-        pl.semaphore_wait(barrier, count)
+        if wait:
+            self.met(count)
+
+    def met(self, count):
+        pl.semaphore_wait(pltpu.get_barrier_semaphore(), count)
 
     def send(self, src, dst, axis, shift):
         index = self.used
@@ -461,22 +465,18 @@
         bufs_xz, bufs_zx,
     )
     ring_p.middle()
-    root_terms(0, 2)
     ring_p.end()
     for item in ga_ps:
         item.start()
     for item in small:
         item.first_ring()
-    root_terms(2, 4)
     for item in small:
         item.first_end()
     for item in large:
         item.first_ring()
-    root_terms(4, 6)
     for a in (0, -1, 1, 2):
         for item in small:
             item.second_ring(a)
-    root_terms(6, 8)
     for item in large:
         item.first_end()
     for item in small:
@@ -489,6 +489,7 @@
         item.first_ring()
     for item in large:
         item.second_ring(0)
+    root_terms(0, 3)
     for item in ga_ps:
         item.first_end()
     ring_ll.middle()
@@ -496,11 +497,13 @@
     for a in (-1, 1):
         for item in large:
             item.second_ring(a)
+    root_terms(3, 5)
     for a in (0, -1, 1):
         for item in ga_ps:
             item.second_ring(a)
     for item in large + ga_ps:
         item.second_ring(2)
+    root_terms(5, 8)
     sc.start()
     sc.plain()
     ring_ll.end()
@@ -509,14 +512,10 @@
     lm_loads = [pltpu.make_async_copy(lm_all.at[k], stage.at[k], load_sem.at[k]) for k in range(MIDS)]
     for load in lm_loads:
         load.start()
-    for item in large + ga_ps:
+    for item in large:
         for a in (0, -1, 1, 2):
             item.second_end(a)
         item.finish()
-    shared_p = []
-    for o in range(4):
-        part = p_all.at[two, pl.ds(128 * o, 128), :]
-        shared_p.append(net.send(part, part, "core", 1))
     spread_m = Spread(net, m_all, um_c, spread_send.at[0], spread_recv.at[0], local_sem.at[6])
     spread_l = Spread(net, r_all, ul_c, spread_send.at[1], spread_recv.at[1], local_sem.at[7])
     spread_m.start()
@@ -539,6 +538,14 @@
 
     ga_m.free()
     mid_nodes(pl.ds(0, 512))
+    for item in ga_ps:
+        for a in (0, -1, 1, 2):
+            item.second_end(a)
+        item.finish()
+    shared_p = []
+    for o in range(4):
+        part = p_all.at[two, pl.ds(128 * o, 128), :]
+        shared_p.append(net.send(part, part, "core", 1))
     sc.middle()
     ring_ll.finish()
     for copy in shared_p:
@@ -700,7 +707,7 @@
 def third_kernel(parent, mid_cross, low_root, um, ul, g, lm, ll, out, terms, lm_t, ll_t, *scratch):
     bufs_xz, bufs_zx, (send_sem, recv_sem) = scratch[:5], scratch[5:10], scratch[10:]
     net = Net(send_sem, recv_sem)
-    net.greet(("x", "z"))
+    net.greet(("x", "z"), wait=False)
     for p in range(MIDS):
         lm_t[p] = jnp.transpose(lm[p])
     for i in range(LOWS):
@@ -733,6 +740,7 @@
         lambda o, h: terms.at[:, o, pl.ds(2 * half + half * h, half), :],
         bufs_xz, bufs_zx,
     )
+    net.met(4)
     sc.start()
     sc.plain()
     sc.middle()

time: 240 us -> 233 us (0.971)
  Pallas kernels: 221 us -> 216 us
    pallas_call x1, Pallas kernels: 34.6 us -> 30.3 us  [third_step(): pl.pallas_call(third_kernel, out_shape=jax.ShapeDtypeStruct((DIAG_ROWS, 1...]
where the time goes in v3:
time: 233 us
  Pallas kernels  216 us (93%)
  other arithmetic  9.62 us (4%)
  local copies, waits for them, and re-layouts  6.87 us (3%)
    pallas_call x1, Pallas kernels, main_step(): pl.pallas_call(main_kernel, out_shape=(shape(512, 256), shape(MIDS, 128,...  185 us
    pallas_call x1, Pallas kernels, third_step(): pl.pallas_call(third_kernel, out_shape=jax.ShapeDtypeStruct((DIAG_ROWS, 1...  30.3 us

profile of v3, /device:TPU:0, one launch (start us, length us, event | category | flops | bytes accessed | tf_op | source)
XLA Modules:
  0.0 232.9 jit_solution(6360270946701215169)
XLA Ops:
  0.7 0.8 compare_reduce_fusion.1
  1.5 0.8 copy.17
  2.3 0.1 compare_reduce_fusion.2
  2.3 0.1 compare_reduce_fusion
  2.5 0.1 iota_compare_fusion.1
  2.6 1.5 multiply_bitcast_fusion.2.p
  4.0 0.1 iota_compare_fusion
  4.2 1.7 broadcast_select_fusion.1.ll
  5.8 1.7 multiply_bitcast_fusion.r
  7.5 1.7 multiply_bitcast_fusion.1.m
  9.2 1.9 broadcast_select_fusion.lm_own.lm
  11.1 185.3 %main_step.1 = (f32[512,256]{1,0:T(8,128)}, f32[2,128,256]{2,1,0:T(8,128)}, f32[4,64,256]{2,1,0:T(8,128)}, f32[4,512,64]{2,1,0:T(8,128)}, f32[2,1024,256]{2,1,0:...) custom-call(s32[4]{0:T(128)} %parent.3, f32[256,4096]{1,0:T(8,128)} %lr.1, ...), custom_call_target="tpu_custom_call" | custom-call | tf_op jit(solution)/shard_map/main_step/pallas_call | solution.py:677
  196.4 0.0 copy-start.2
  196.4 0.0 copy-start.1
  196.5 0.0 copy-start
  196.5 30.3 %third_step.1 = f32[320,128]{1,0:T(8,128)} custom-call(s32[4]{0:T(128)} %parent.3, f32[2,128,256]{2,1,0:T(8,128)} %get-tuple-element.30.mid_cross, f32[4,64,256]{2,1,0:T(8,128)} %get-tuple-element.33.low_root, f32[2,1024,256]{2,1,0:T(8,128)} %get-tuple-element.15.um, f32[4,512,256]{2,1,0:T(8,128)} %get-tuple-element.16.ul, ...), custom_call_target="tpu_custom_call" | custom-call | tf_op jit(solution)/shard_map/third_step/pallas_call | solution.py:754
  226.8 0.8 slice.10
  227.5 1.5 fusion.3
  229.0 0.1 reshape.106
  229.1 0.6 copy.19
  229.8 0.1 reshape.108
  229.9 0.8 copy.20
  230.7 0.0 copy-done.2
  230.7 0.8 copy.24
  231.5 0.0 copy-done.1
  231.5 0.7 copy.25
  232.2 0.0 copy-done
  232.2 0.7 copy.26
  (7 shorter events, 0.1 us)
Async XLA Ops:
  196.4 34.2 %copy-start.2 = (f32[512,256]{1,0:T(8,128)S(1)}, f32[512,256]{1,0:T(8,128)}, u32[]{:S(2)}) copy-start(f32[512,256]{1,0:T(8,128)} %get-tuple-element.28) | copy-start | bytes 1572868
  196.4 35.0 %copy-start.1 = (f32[2,128,256]{2,1,0:T(8,128)S(1)}, f32[2,128,256]{2,1,0:T(8,128)}, u32[]{:S(2)}) copy-start(f32[2,128,256]{2,1,0:T(8,128)} %get-tuple-element.30.mid_cross) | copy-start | bytes 786436
  196.5 35.7 %copy-start = (f32[4,64,256]{2,1,0:T(8,128)S(1)}, f32[4,64,256]{2,1,0:T(8,128)}, u32[]{:S(2)}) copy-start(f32[4,64,256]{2,1,0:T(8,128)} %get-tuple-element.33.low_root) | copy-start | bytes 786436
